TPU v7x, 32 devices: a whole 2x2x4 slice. The times are simulated.
32 devices in a mesh: grp: 4 (over y, core), ctx: 8 (over z, x).
Axes of the slice: x: 2, y: 2, z: 4, core: 2. Of those that a mesh axis runs over, the one named last changes fastest.
Arguments:
- query_rows: bfloat16 [4, 1024, 4096], P('grp', 'ctx'), may hold values from -6 to 6
- key_rows: bfloat16 [4, 1024, 512], P('grp', 'ctx'), may hold values from -6 to 6
- value_rows: bfloat16 [4, 1024, 512], P('grp', 'ctx'), may hold values from -5 to 5
- output_rows: bfloat16 [4, 1024, 4096], P('grp', 'ctx'), may hold values from -4 to 4
- output_grad: bfloat16 [4, 1024, 4096], P('grp', 'ctx'), may hold values from -5 to 5
- loss_mask: int32 [4, 1024], P('grp', 'ctx'), may hold values from 0 to 1
- doc_lengths: int32 [4, 12], P('grp'), may hold values from 1 to 256, 1024 in all within a row
- balance_plan: int32 [4, 128], P('grp'), may hold values from 0 to 127, as said below
Outputs:
- query_grad: bfloat16 [4, 1024, 4096], P('grp', 'ctx')
- key_grad: bfloat16 [4, 1024, 512], P('grp', 'ctx')
- value_grad: bfloat16 [4, 1024, 512], P('grp', 'ctx')
Inputs may be any that keep to these rules, and one draw needn't show every extreme that they name: Each row is a permutation of 0 to 127. Span c of a sequence (its tokens c * 8 to c * 8 + 7) goes to index balance_plan // 16 of ctx; of the 16 spans of one index of ctx at most 2 go to the same index.
All inputs are finite; a program needn't handle non-finite values.
Results may differ from a plain program's by a relative error of at most 0.0051.
Values may be sent and summed in bfloat16 or wider, within the bound.
A program may use at most 128 MiB of HBM per device.

v0:
```python
import jax
import jax.numpy as jnp
from jax import lax
from jax.sharding import PartitionSpec as P

HD = 128
QH = 32
KVH = 4
SPAN = 8
NEGATIVE = -1e30


def key_block():
    return 512


def doc_index(positions, doc_ends):
    return jnp.sum((positions[:, None] >= doc_ends[None, :]).astype(jnp.int32), axis=1)


def visible(query_pos, query_doc, key_pos, doc_ends):
    key_doc = doc_index(key_pos, doc_ends)
    return (key_pos[None, :] <= query_pos[:, None]) & (key_doc[None, :] == query_doc[:, None])


def head_scores(q_heads, k_heads, scale_value):
    return (
        jnp.einsum("rgsd,ngd->gsrn", q_heads, k_heads, preferred_element_type=jnp.float32)
        * scale_value
    )


def over_blocks(function, folded, members):
    row_total = members[0].shape[0]
    block_rows = key_block()
    step_count = row_total // block_rows
    stacked = tuple(
        (member.reshape((step_count, block_rows) + member.shape[1:]) for member in members)
    )

    def advance(carried, scanned):
        block_index, pieces = scanned
        positions = block_index * block_rows + jnp.arange(block_rows, dtype=jnp.int32)
        return (function(carried, pieces, positions), None)

    result, unused = lax.scan(advance, folded, (jnp.arange(step_count, dtype=jnp.int32), stacked))
    return result


def stats_update(carried, k_heads, key_pos, context):
    q_heads, query_pos, query_doc, doc_ends, scale_value = context
    old_peak, running_sum = carried
    scores = head_scores(q_heads, k_heads, scale_value)
    visible_mask = visible(query_pos, query_doc, key_pos, doc_ends)
    scores = jnp.where(visible_mask, scores, NEGATIVE)
    new_peak = jnp.maximum(old_peak, jnp.max(scores, axis=-1))
    weights = jnp.where(visible_mask, jnp.exp(scores - new_peak[..., None]), 0.0)
    running_sum = running_sum * jnp.exp(old_peak - new_peak) + jnp.sum(weights, axis=-1)
    return (new_peak, running_sum)


def block_grads(context, k_heads, v_heads, key_pos):
    q_heads, g_heads, query_pos, query_doc, doc_ends, lse_rows, delta_heads, scale_value = context
    scores = head_scores(q_heads, k_heads, scale_value)
    visible_mask = visible(query_pos, query_doc, key_pos, doc_ends)
    probs_full = jnp.where(
        visible_mask, jnp.exp(jnp.where(visible_mask, scores - lse_rows[..., None], NEGATIVE)), 0.0
    )
    probs_half = probs_full.astype(jnp.bfloat16)
    dprobs = jnp.einsum("rgsd,ngd->gsrn", g_heads, v_heads, preferred_element_type=jnp.float32)
    dscores = (probs_full * (dprobs - delta_heads[..., None]) * scale_value).astype(jnp.bfloat16)
    query_part = jnp.einsum("gsrn,ngd->rgsd", dscores, k_heads, preferred_element_type=jnp.float32)
    key_part = jnp.einsum("gsrn,rgsd->ngd", dscores, q_heads, preferred_element_type=jnp.float32)
    value_part = jnp.einsum(
        "gsrn,rgsd->ngd", probs_half, g_heads, preferred_element_type=jnp.float32
    )
    return (query_part, key_part, value_part)


def row_delta(grad_local, output_local):
    local_rows = grad_local.shape[0]
    product = grad_local.astype(jnp.float32) * output_local.astype(jnp.float32)
    return jnp.sum(product.reshape(local_rows, QH, HD), axis=-1)


def shards(
    query_rows, key_rows, value_rows, output_rows, output_grad, loss_mask, doc_lengths, balance_plan
):
    devices = lax.axis_size("ctx")
    device = lax.axis_index("ctx")
    local_rows = query_rows.shape[1]
    per_device = local_rows // SPAN
    slot_count = (per_device + devices - 1) // devices
    group_size = QH // KVH
    scale_value = HD ** (-0.5)
    counted = jnp.sum(loss_mask.astype(jnp.float32))
    total_counted = lax.psum(counted, ("grp", "ctx"))
    factor = lax.axis_size("grp") * devices * local_rows / jnp.maximum(total_counted, 1.0)
    grad_masked = output_grad[0] * loss_mask[0][:, None].astype(jnp.bfloat16)
    plan_row = balance_plan[0]
    dest_all = plan_row // per_device
    dest_grid = dest_all.reshape(devices, per_device)
    earlier = jnp.arange(per_device)[None, :] < jnp.arange(per_device)[:, None]
    same_dest = dest_grid[:, :, None] == dest_grid[:, None, :]
    rank_all = jnp.sum((same_dest & earlier[None, :, :]).astype(jnp.int32), axis=2).reshape(-1)
    inverse = jnp.argsort(plan_row)
    handled = lax.dynamic_slice_in_dim(inverse, device * per_device, per_device)
    receive_index = handled // per_device * slot_count + jnp.take(rank_all, handled)
    send_dest = lax.dynamic_slice_in_dim(dest_all, device * per_device, per_device)
    send_rank = lax.dynamic_slice_in_dim(rank_all, device * per_device, per_device)
    send_index = send_dest * slot_count + send_rank

    def pack_rows(member):
        row_width = member.shape[-1]
        pieces = member.reshape(per_device, SPAN, row_width)
        buffer = jnp.zeros((devices * slot_count, SPAN, row_width), member.dtype)
        return buffer.at[send_index].set(pieces)

    def unpack(member):
        return jnp.take(member, receive_index, axis=0).reshape(local_rows, member.shape[-1])

    moved_query, moved_grad, moved_output = (
        lax.all_to_all(pack_rows(query_rows[0]), "ctx", split_axis=0, concat_axis=0, tiled=True),
        lax.all_to_all(pack_rows(grad_masked), "ctx", split_axis=0, concat_axis=0, tiled=True),
        lax.all_to_all(pack_rows(output_rows[0]), "ctx", split_axis=0, concat_axis=0, tiled=True),
    )
    delta_rows = row_delta(unpack(moved_grad), unpack(moved_output))
    q_local = unpack(moved_query)
    g_local = unpack(moved_grad)
    q_heads = q_local.reshape(local_rows, KVH, group_size, HD)
    g_heads = g_local.reshape(local_rows, KVH, group_size, HD)
    delta_heads = jnp.transpose(delta_rows).reshape(KVH, group_size, local_rows)
    query_pos = (handled[:, None] * SPAN + jnp.arange(SPAN, dtype=jnp.int32)[None, :]).reshape(
        local_rows
    )
    doc_ends = jnp.cumsum(doc_lengths[0])
    query_doc = doc_index(query_pos, doc_ends)
    stats_context = (q_heads, query_pos, query_doc, doc_ends, scale_value)
    stats_initial = (
        jnp.full((KVH, group_size, local_rows), NEGATIVE, jnp.float32),
        jnp.zeros((KVH, group_size, local_rows), jnp.float32),
    )

    def stats_step_rows(carried, members, positions):
        return stats_update(carried, members[0].reshape(-1, KVH, HD), positions, stats_context)

    peak_rows, sum_rows = over_blocks(
        stats_step_rows, stats_initial, (lax.all_gather(key_rows, "ctx", axis=1, tiled=True)[0],)
    )
    lse_rows = peak_rows + jnp.log(sum_rows)
    grad_context = (
        q_heads,
        g_heads,
        query_pos,
        query_doc,
        doc_ends,
        lse_rows,
        delta_heads,
        scale_value,
    )
    dq_zero = jnp.zeros((local_rows, KVH, group_size, HD), jnp.float32)
    seq_total = local_rows * devices
    grads_initial = (
        dq_zero,
        jnp.zeros((seq_total, KVH, HD), jnp.float32),
        jnp.zeros((seq_total, KVH, HD), jnp.float32),
    )

    def grads_step_rows(carried, members, positions):
        dq_acc, dk_all, dv_all = carried
        k_heads = members[0].reshape(-1, KVH, HD)
        v_heads = members[1].reshape(-1, KVH, HD)
        query_part, key_part, value_part = block_grads(grad_context, k_heads, v_heads, positions)
        first_row = positions[0]
        old_keys = lax.dynamic_slice_in_dim(dk_all, first_row, key_part.shape[0], 0)
        dk_all = lax.dynamic_update_slice_in_dim(dk_all, old_keys + key_part, first_row, 0)
        old_values = lax.dynamic_slice_in_dim(dv_all, first_row, value_part.shape[0], 0)
        dv_all = lax.dynamic_update_slice_in_dim(dv_all, old_values + value_part, first_row, 0)
        return (dq_acc + query_part, dk_all, dv_all)

    dq_sum, dk_all, dv_all = over_blocks(
        grads_step_rows,
        grads_initial,
        (
            lax.all_gather(key_rows, "ctx", axis=1, tiled=True)[0],
            lax.all_gather(value_rows, "ctx", axis=1, tiled=True)[0],
        ),
    )
    dk_mine, dv_mine = (
        lax.psum_scatter(dk_all, "ctx", scatter_dimension=0, tiled=True),
        lax.psum_scatter(dv_all, "ctx", scatter_dimension=0, tiled=True),
    )
    query_grad = (dq_sum * factor).astype(jnp.bfloat16).reshape(1, local_rows, QH * HD)
    key_grad = (dk_mine * factor).astype(jnp.bfloat16).reshape(1, local_rows, KVH * HD)
    value_grad = (dv_mine * factor).astype(jnp.bfloat16).reshape(1, local_rows, KVH * HD)
    return (query_grad, key_grad, value_grad)


def solution(mesh):
    in_specs = (
        P("grp", "ctx", None),
        P("grp", "ctx", None),
        P("grp", "ctx", None),
        P("grp", "ctx", None),
        P("grp", "ctx", None),
        P("grp", "ctx"),
        P("grp", None),
        P("grp", None),
    )
    out_specs = (P("grp", "ctx", None), P("grp", "ctx", None), P("grp", "ctx", None))
    return jax.shard_map(shards, mesh=mesh, in_specs=in_specs, out_specs=out_specs, check_vma=False)
```

profile of v0, /device:TPU:0, one launch (start us, length us, event | category | flops | bytes accessed | tf_op | source)
XLA Modules:
  0.0 347.5 jit_solution(4692239312249407797)
XLA Ops:
  7.2 0.7 and_select_fusion.2
  8.4 1.3 reduce.7
  10.3 1.1 broadcast.162.clone.1
  11.4 3.4 scatter_fusion
  14.8 7.2 %all-to-all-start = ((bf16[16,8,4096]{2,1,0:T(8,128)(2,1)}), bf16[16,8,4096]{2,1,0:T(8,128)(2,1)S(1)}, u32[]{:S(2)}, u32[]{:S(2)}) async-start(bf16[16,8,4096]{2,1,0:T(8,128)(2,1)} %scatter_fusion), calls=%async_computation | async-start | bytes 2097152 | tf_op jit(solution)/shard_map/all_to_all | solution.py:123
  22.1 0.7 all-gather.3.cloned.1.call-update
  22.8 0.7 convert_reduce_fusion.5
  23.6 1.4 bitcast_multiply_fusion
  25.0 1.1 broadcast.162.clone
  26.0 2.9 scatter_fusion.1
  29.0 23.0 %all-to-all-done = bf16[16,8,4096]{2,1,0:T(8,128)(2,1)S(1)} async-done(((bf16[16,8,4096]{2,1,0:T(8,128)(2,1)}), bf16[16,8,4096]{2,1,0:T(8,128)(2,1)S(1)}, u32[]{:S(2)}, u32[]{:S(2)}) %all-to-all-start) | async-done | bytes 1048608 | tf_op jit(solution)/shard_map/all_to_all | solution.py:123
  52.0 4.2 %all-to-all-start.1 = ((bf16[16,8,4096]{2,1,0:T(8,128)(2,1)}), bf16[16,8,4096]{2,1,0:T(8,128)(2,1)}, u32[]{:S(2)}, u32[]{:S(2)}) async-start(bf16[16,8,4096]{2,1,0:T(8,128)(2,1)} %scatter_fusion.1), calls=%async_computation.1 | async-start | bytes 2097152 | tf_op jit(solution)/shard_map/all_to_all | solution.py:124
  56.3 0.7 all-gather.5.cloned.1.call-update
  57.2 2.5 sort.17
  59.9 0.7 gather_fusion
  60.7 1.1 broadcast.162.clone.2
  61.8 3.4 scatter_fusion.2
  65.4 21.0 %all-gather.3.cloned.1.call-done = bf16[1,1024,512]{2,1,0:T(8,128)(2,1)} async-done(((bf16[1,128,512]{2,1,0:T(8,128)(2,1)}), bf16[1,1024,512]{2,1,0:T(8,128)(2,1)}) %all-gather.3.cloned.1.call-update) | async-done | bytes 1048592 | tf_op jit(solution)/shard_map/all_gather | solution.py:185
  86.4 1.5 copy.59
  87.9 0.6 gather_fusion.1
  88.5 1.6 all-to-all-done.1
  90.1 4.2 %all-to-all-start.2 = ((bf16[16,8,4096]{2,1,0:T(8,128)(2,1)}), bf16[16,8,4096]{2,1,0:T(8,128)(2,1)}, u32[]{:S(2)}, u32[]{:S(2)}) async-start(bf16[16,8,4096]{2,1,0:T(8,128)(2,1)} %scatter_fusion.2), calls=%async_computation.2 | async-start | bytes 2097152 | tf_op jit(solution)/shard_map/all_to_all | solution.py:125
  94.4 1.8 gather_fusion.2
  96.2 1.2 fusion.26
  98.1 10.8 %while.28 = (s32[]{:T(128)}, f32[4,8,128]{2,1,0:T(8,128)S(1)}, f32[4,8,128]{2,1,0:T(8,128)S(1)}, s32[2]{0:T(128)S(1)}, s32[12]{0:T(128)S(1)}, /*index=5*/s32[128...) while((s32[]{:T(128)}, f32[4,8,128]{2,1,0:T(8,128)S(1)}, ...), condition=%wide.region_9.11_spmd.clone, body=%wide.region_5.10_spmd.clone.sunk | while | flops 553883776 | bytes 19821336 | solution.py:46
  99.9 1.5 fusion.62
  101.3 2.1 select_reduce_fusion.2
  105.3 1.5 fusion.62
  106.7 2.1 select_reduce_fusion.2
  108.9 1.4 copy.83
  110.3 1.4 copy.62
  111.7 17.6 %all-to-all-done.2 = bf16[16,8,4096]{2,1,0:T(8,128)(2,1)} async-done(((bf16[16,8,4096]{2,1,0:T(8,128)(2,1)}), bf16[16,8,4096]{2,1,0:T(8,128)(2,1)}, u32[]{:S(2)}, u32[]{:S(2)}) %all-to-all-start.2) | async-done | bytes 1048608 | tf_op jit(solution)/shard_map/all_to_all | solution.py:125
  129.3 2.8 gather_fusion.3
  132.2 1.6 multiply_bitcast_fusion
  133.8 1.7 copy.84
  135.5 2.2 reduce_sum.65
  137.8 1.5 broadcast.160.clone
  139.3 1.4 broadcast.160
  140.7 59.4 %while.29 = (s32[]{:T(128)}, f32[128,4,8,128]{0,3,2,1:T(8,128)}, f32[1024,4,128]{2,0,1:T(8,128)}, f32[1024,4,128]{2,0,1:T(8,128)}, bf16[2,512,512]{1,2,0:T(8,128...) while((s32[]{:T(128)}, f32[128,4,8,128]{0,3,2,1:T(8,128)}, ...), condition=%wide.region_15.17_spmd.clone, body=%wide.region_13.16_spmd.clone.sunk | while | flops 2713405440 | bytes 80475096 | solution.py:46
  144.9 1.1 constant_dynamic-slice_fusion.8
  146.3 1.3 fusion.74
  148.0 3.1 fusion.77
  151.1 3.5 %fusion.75 = bf16[4,8,128,512]{2,3,1,0:T(8,128)(2,1)S(1)} fusion(f32[4,512,128,8]{2,1,3,0:T(8,128)S(1)} %fusion.74, f32[4,8,128]{2,1,0:T(8,128)S(1)} %bitcast.176, f32[4,8,128]{2,1,0:T(8,128)S(1)} %get-tuple-element.587, pred[128,512]{0,1:T(8,128)(4,1)S(1)} %compare_and_fusion.6, bf16[512,4,128,1]{0,2,3,1:T(8,128)(2,1)S(1)} %bitcast.164, ...), kind=kOutput, calls=%fused_computation.23.clone.1 | convolution fusion | flops 553648128 | bytes 14254080 | tf_op jit(solution)/shard_map/while/body/eval_jaxpr/rgsd,ngd->gsrn/dot_general | solution.py:70
  154.7 1.3 fusion.76
  156.0 2.3 bitcast_add_fusion.2
  158.2 5.9 %dynamic_update_slice.10 = f32[1024,4,128]{2,0,1:T(8,128)} dynamic-update-slice(f32[1024,4,128]{2,0,1:T(8,128)} %get-tuple-element.562, f32[512,4,128]{2,0,1:T(8,128)S(1)} %fusion.76, s32[]{:T(128)S(6)} %select_n.158, s32[]{:T(128)} %constant.75.clone.1..sunk.1, s32[]{:T(128)} %constant.75.clone.1..sunk.1) | dynamic-update-slice | bytes 2097156 | tf_op jit(solution)/shard_map/while/body/eval_jaxpr/dynamic_update_slice | solution.py:176
  164.1 6.2 %dynamic_update_slice.11 = f32[1024,4,128]{2,0,1:T(8,128)} dynamic-update-slice(f32[1024,4,128]{2,0,1:T(8,128)} %get-tuple-element.563, f32[512,4,128]{2,0,1:T(8,128)} %fusion.77, s32[]{:T(128)S(6)} %select_n.158, s32[]{:T(128)} %constant.75.clone.1..sunk.1, s32[]{:T(128)} %constant.75.clone.1..sunk.1) | dynamic-update-slice | bytes 2097156 | tf_op jit(solution)/shard_map/while/body/eval_jaxpr/dynamic_update_slice | solution.py:178
  174.5 1.1 constant_dynamic-slice_fusion.8
  175.9 1.3 fusion.74
  177.7 3.1 fusion.77
  180.7 3.5 %fusion.75 = bf16[4,8,128,512]{2,3,1,0:T(8,128)(2,1)S(1)} fusion(f32[4,512,128,8]{2,1,3,0:T(8,128)S(1)} %fusion.74, f32[4,8,128]{2,1,0:T(8,128)S(1)} %bitcast.176, f32[4,8,128]{2,1,0:T(8,128)S(1)} %get-tuple-element.587, pred[128,512]{0,1:T(8,128)(4,1)S(1)} %compare_and_fusion.6, bf16[512,4,128,1]{0,2,3,1:T(8,128)(2,1)S(1)} %bitcast.164, ...), kind=kOutput, calls=%fused_computation.23.clone.1 | convolution fusion | flops 553648128 | bytes 14254080 | tf_op jit(solution)/shard_map/while/body/eval_jaxpr/rgsd,ngd->gsrn/dot_general | solution.py:70
  184.3 1.3 fusion.76
  185.6 3.9 %bitcast_add_fusion.2 = f32[128,4,8,128]{0,3,2,1:T(8,128)} fusion(f32[128,4,8,128]{0,3,2,1:T(8,128)} %get-tuple-element.561, bf16[512,4,128,1]{0,2,3,1:T(8,128)(2,1)S(1)} %bitcast.162, bf16[4,8,128,512]{2,3,1,0:T(8,128)(2,1)S(1)} %fusion.75, pred[]{:T(512)S(6)} %compare.25), kind=kOutput, calls=%fused_computation.31.clone.1 | convolution fusion | flops 537919488 | bytes 8912897 | tf_op jit(solution)/shard_map/while/body/eval_jaxpr/gsrn,ngd->rgsd/dot_general | solution.py:72
  189.4 5.2 %dynamic_update_slice.10 = f32[1024,4,128]{2,0,1:T(8,128)} dynamic-update-slice(f32[1024,4,128]{2,0,1:T(8,128)} %get-tuple-element.562, f32[512,4,128]{2,0,1:T(8,128)S(1)} %fusion.76, s32[]{:T(128)S(6)} %select_n.158, s32[]{:T(128)} %constant.75.clone.1..sunk.1, s32[]{:T(128)} %constant.75.clone.1..sunk.1) | dynamic-update-slice | bytes 2097156 | tf_op jit(solution)/shard_map/while/body/eval_jaxpr/dynamic_update_slice | solution.py:176
  194.6 5.5 %dynamic_update_slice.11 = f32[1024,4,128]{2,0,1:T(8,128)} dynamic-update-slice(f32[1024,4,128]{2,0,1:T(8,128)} %get-tuple-element.563, f32[512,4,128]{2,0,1:T(8,128)} %fusion.77, s32[]{:T(128)S(6)} %select_n.158, s32[]{:T(128)} %constant.75.clone.1..sunk.1, s32[]{:T(128)} %constant.75.clone.1..sunk.1) | dynamic-update-slice | bytes 2097156 | tf_op jit(solution)/shard_map/while/body/eval_jaxpr/dynamic_update_slice | solution.py:178
  200.8 0.6 convert_reduce_fusion.4
  201.4 40.0 %psum.7 = f32[]{:T(128)} all-reduce(f32[]{:T(128)} %convert_reduce_fusion.4), channel_id=1, replica_groups=mesh['grp'=4,'ctx'=8] {'grp','ctx'}, use_global_device_ids=true, to_apply=%region_17.19 | all-reduce | flops 1 | bytes 8 | tf_op jit(solution)/shard_map/psum | solution.py:97
  242.0 1.9 multiply_convert_fusion
  243.9 1.3 copy.74
  245.2 22.4 %reduce-scatter.5.cloned.1.call-done = f32[128,4,128]{2,0,1:T(8,128)} async-done(((f32[1024,4,128]{2,0,1:T(8,128)}), f32[128,4,128]{2,0,1:T(8,128)}) %reduce-scatter.5.cloned.1.call-update) | async-done | bytes 262160 | tf_op jit(solution)/shard_map/reduce_scatter | solution.py:191
  267.6 70.6 %reduce-scatter.3.cloned.1.call-done = f32[128,4,128]{2,0,1:T(8,128)} async-done(((f32[1024,4,128]{2,0,1:T(8,128)}), f32[128,4,128]{2,0,1:T(8,128)}) %reduce-scatter.3.cloned.1.call-update) | async-done | bytes 262160 | tf_op jit(solution)/shard_map/reduce_scatter | solution.py:190
  338.2 1.1 multiply_convert_fusion.1
  339.4 0.7 reshape.207
  340.2 0.7 reshape.206
  (91 shorter events, 10.3 us)
Async XLA Ops:
  7.2 50.1 %copy-start.4 = (s32[1,128]{1,0:T(1,128)S(1)}, s32[1,128]{1,0:T(1,128)}, u32[]{:S(2)}) copy-start(s32[1,128]{1,0:T(1,128)} %param.21) | copy-start | bytes 1540
  7.2 49.9 %copy-start.3 = (s32[1,12]{1,0:T(1,128)S(1)}, s32[1,12]{1,0:T(1,128)}, u32[]{:S(2)}) copy-start(s32[1,12]{1,0:T(1,128)} %param.20) | copy-start | bytes 148
  14.8 37.2 %all-to-all-start = ((bf16[16,8,4096]{2,1,0:T(8,128)(2,1)}), bf16[16,8,4096]{2,1,0:T(8,128)(2,1)S(1)}, u32[]{:S(2)}, u32[]{:S(2)}) async-start(bf16[16,8,4096]{2,1,0:T(8,128)(2,1)} %scatter_fusion), calls=%async_computation | async-start | bytes 2097152 | tf_op jit(solution)/shard_map/all_to_all | solution.py:123
  22.1 64.3 %all-gather.3.cloned.1.call-start = ((), (), s32[]{:S(2)}) async-start(), calls=%async_computation.5 | async-start | bytes 1179648 | tf_op jit(solution)/shard_map/all_gather | solution.py:185
  52.0 38.1 %all-to-all-start.1 = ((bf16[16,8,4096]{2,1,0:T(8,128)(2,1)}), bf16[16,8,4096]{2,1,0:T(8,128)(2,1)}, u32[]{:S(2)}, u32[]{:S(2)}) async-start(bf16[16,8,4096]{2,1,0:T(8,128)(2,1)} %scatter_fusion.1), calls=%async_computation.1 | async-start | bytes 2097152 | tf_op jit(solution)/shard_map/all_to_all | solution.py:124
  56.3 81.5 %all-gather.5.cloned.1.call-start = ((), (), s32[]{:S(2)}) async-start(), calls=%async_computation.6 | async-start | bytes 1179648 | tf_op jit(solution)/shard_map/all_gather | solution.py:186
  90.1 39.3 %all-to-all-start.2 = ((bf16[16,8,4096]{2,1,0:T(8,128)(2,1)}), bf16[16,8,4096]{2,1,0:T(8,128)(2,1)}, u32[]{:S(2)}, u32[]{:S(2)}) async-start(bf16[16,8,4096]{2,1,0:T(8,128)(2,1)} %scatter_fusion.2), calls=%async_computation.2 | async-start | bytes 2097152 | tf_op jit(solution)/shard_map/all_to_all | solution.py:125
  94.3 173.3 %reduce-scatter.5.cloned.1.call-start = ((), (), s32[]{:S(2)}) async-start(), calls=%async_computation.8 | async-start | bytes 2359296 | tf_op jit(solution)/shard_map/reduce_scatter | solution.py:191
  140.7 60.0 %copy-start.5 = (s32[1,128]{1,0:T(1,128)S(1)}, s32[1,128]{1,0:T(1,128)}, u32[]{:S(2)}) copy-start(s32[1,128]{1,0:T(1,128)} %param.19) | copy-start | bytes 1540
  146.2 1.6 copy-start.1
  146.2 1.8 copy-start.2
  151.1 3.6 %copy-start = (f32[1024,4,128]{2,0,1:T(8,128)S(1)}, f32[1024,4,128]{2,0,1:T(8,128)}, u32[]{:S(2)}) copy-start(f32[1024,4,128]{2,0,1:T(8,128)} %get-tuple-element.562) | copy-start | bytes 6291460 | tf_op jit(solution)/shard_map/while
  175.8 1.6 copy-start.1
  175.8 1.8 copy-start.2
  180.7 3.6 %copy-start = (f32[1024,4,128]{2,0,1:T(8,128)S(1)}, f32[1024,4,128]{2,0,1:T(8,128)}, u32[]{:S(2)}) copy-start(f32[1024,4,128]{2,0,1:T(8,128)} %get-tuple-element.562) | copy-start | bytes 6291460 | tf_op jit(solution)/shard_map/while
  200.2 138.1 %reduce-scatter.3.cloned.1.call-start = ((), (), s32[]{:S(2)}) async-start(), calls=%async_computation.7 | async-start | bytes 2359296 | tf_op jit(solution)/shard_map/reduce_scatter | solution.py:190
Sparse Core Ops, SparseCore 0:
  25.0 61.2 all-gather.2
  88.5 45.8 all-gather.4
  200.3 67.3 reduce-scatter.4
  271.0 67.1 reduce-scatter.2
where the time goes:
time: 349 us; the launch traced here: 347 us
  waiting for transfers between devices  158 us (45%)
  local copies, waits for them, and re-layouts  62.7 us (18%)
  blocking collectives  40 us (11%)
  matrix products  27.4 us (8%)
  other arithmetic  21.9 us (6%)
  starting transfers between devices  15.9 us (5%)
  between operations  14.7 us (4%)
  loops' own time  6.75 us (2%)
    reduce_scatter x1, waiting for transfers between devices, shards(): lax.psum_scatter(dk_all, 'ctx', scatter_dimension=0, tiled=True)  70.6 us
    psum x1, blocking collectives, shards(): total_counted = lax.psum(counted, ('grp', 'ctx'))  40 us
    all_to_all x1, waiting for transfers between devices, shards(): lax.all_to_all(pack_rows(query_rows[0]), 'ctx', split_axis=0, concat_axis...  23 us
    reduce_scatter x1, waiting for transfers between devices, shards(): lax.psum_scatter(dv_all, 'ctx', scatter_dimension=0, tiled=True)  22.4 us
    all_gather x1, waiting for transfers between devices, shards(): lax.all_gather(key_rows, 'ctx', axis=1, tiled=True)[0]  21 us
    all_to_all x1, waiting for transfers between devices, shards(): lax.all_to_all(pack_rows(output_rows[0]), 'ctx', split_axis=0, concat_axi...  17.6 us
    dynamic_update_slice x2, local copies, waits for them, and re-layouts, grads_step_rows(): lax.dynamic_update_slice_in_dim(dv_all, old_values + value_part, first_ro...  11.7 us
    dynamic_update_slice x2, local copies, waits for them, and re-layouts, grads_step_rows(): lax.dynamic_update_slice_in_dim(dk_all, old_keys + key_part, first_row, 0)  11.1 us
  transfers between devices with their start and end apart: 7, of which 6 were waited for; matrix products, arithmetic and copies ran while one was open for 13% of the time, Pallas kernels for 0%

commit v1 on v0

--- a/solution.py
+++ b/solution.py
@@ -8,6 +8,28 @@
 KVH = 4
 SPAN = 8
 NEGATIVE = -1e30
+
+
+def laid_out(blocks, dim):
+    blocks = jnp.moveaxis(blocks, 0, dim)
+    shape = blocks.shape
+    return blocks.reshape(*shape[:dim], shape[dim] * shape[dim + 1], *shape[dim + 2 :])
+
+
+def grow_blocks(x, axis):
+    size = lax.axis_size(axis)
+    blocks = x[None]
+    for level in range(size.bit_length() - 1):
+        bit = 1 << level
+        other = lax.ppermute(blocks, axis, [(i, i ^ bit) for i in range(size)])
+        both = jnp.stack([blocks, other])
+        upper = lax.axis_index(axis) >> level & 1
+        blocks = jnp.where(upper == 0, both, both[::-1]).reshape(-1, *x.shape)
+    return blocks
+
+
+def gather_by_bits(x, axis, dim):
+    return laid_out(grow_blocks(x, axis), dim)
 
 
 def key_block():
@@ -182,7 +204,7 @@
         grads_step_rows,
         grads_initial,
         (
-            lax.all_gather(key_rows, "ctx", axis=1, tiled=True)[0],
+            gather_by_bits(key_rows, "ctx", 1)[0],
             lax.all_gather(value_rows, "ctx", axis=1, tiled=True)[0],
         ),
     )

time: 349 us -> 375 us (1.074)
  waiting for transfers between devices: 158 us -> 176 us
  starting transfers between devices: 15.9 us -> 24 us
    ppermute x0 -> x3, waiting for transfers between devices: none -> 48.1 us  [grow_blocks(): other = lax.ppermute(blocks, axis, [(i, i ^ bit) for i in range(size)])]
    all_gather x1, waiting for transfers between devices: 21 us -> 0.02 us  [shards(): lax.all_gather(key_rows, 'ctx', axis=1, tiled=True)[0]]
    all_to_all x1, waiting for transfers between devices: 17.6 us -> 5.58 us  [shards(): lax.all_to_all(pack_rows(output_rows[0]), 'ctx', split_axis=0, concat_axi...]
    ppermute x0 -> x3, starting transfers between devices: none -> 8.58 us  [grow_blocks(): other = lax.ppermute(blocks, axis, [(i, i ^ bit) for i in range(size)])]
    dynamic_slice x12 -> x14, local copies, waits for them, and re-layouts: 5.12 us -> 10.1 us  [over_blocks(): lax.scan(advance, folded, (jnp.arange(step_count, dtype=jnp.int32), stack...]
    another operation x5 -> x7, local copies, waits for them, and re-layouts: 6.16 us -> 8.49 us
  transfers between devices with their start and end apart: 7 -> 10, of which waited for: 6 -> 6; matrix products, arithmetic and copies ran while one was open for 13% -> 15% of each run, Pallas kernels for 0% -> 0%
where the time goes in v1:
time: 375 us; the launch traced here: 373 us
  waiting for transfers between devices  176 us (47%)
  local copies, waits for them, and re-layouts  65.8 us (18%)
  blocking collectives  38.4 us (10%)
  matrix products  25.5 us (7%)
  starting transfers between devices  24 us (6%)
  other arithmetic  21.8 us (6%)
  between operations  14.8 us (4%)
  loops' own time  6.95 us (2%)
    reduce_scatter x1, waiting for transfers between devices, shards(): lax.psum_scatter(dk_all, 'ctx', scatter_dimension=0, tiled=True)  70.6 us
    ppermute x3, waiting for transfers between devices, grow_blocks(): other = lax.ppermute(blocks, axis, [(i, i ^ bit) for i in range(size)])  48.1 us
    psum x1, blocking collectives, shards(): total_counted = lax.psum(counted, ('grp', 'ctx'))  38.4 us
    all_to_all x1, waiting for transfers between devices, shards(): lax.all_to_all(pack_rows(query_rows[0]), 'ctx', split_axis=0, concat_axis...  26.3 us
    reduce_scatter x1, waiting for transfers between devices, shards(): lax.psum_scatter(dv_all, 'ctx', scatter_dimension=0, tiled=True)  24.1 us
    dynamic_update_slice x2, local copies, waits for them, and re-layouts, grads_step_rows(): lax.dynamic_update_slice_in_dim(dk_all, old_keys + key_part, first_row, 0)  11.1 us
    dynamic_update_slice x2, local copies, waits for them, and re-layouts, grads_step_rows(): lax.dynamic_update_slice_in_dim(dv_all, old_values + value_part, first_ro...  11.1 us
    dynamic_slice x14, local copies, waits for them, and re-layouts, over_blocks(): lax.scan(advance, folded, (jnp.arange(step_count, dtype=jnp.int32), stack...  10.1 us
  transfers between devices with their start and end apart: 10, of which 6 were waited for; matrix products, arithmetic and copies ran while one was open for 15% of the time, Pallas kernels for 0%

profile of v1, /device:TPU:0, one launch (start us, length us, event | category | flops | bytes accessed | tf_op | source)
XLA Modules:
  0.0 373.2 jit_solution(17545075769265312705)
XLA Ops:
  8.5 1.3 reduce.7
  11.0 1.1 broadcast.168.clone.1
  12.1 3.4 scatter_fusion
  15.4 7.3 %all-to-all-start = ((bf16[16,8,4096]{2,1,0:T(8,128)(2,1)}), bf16[16,8,4096]{2,1,0:T(8,128)(2,1)S(1)}, u32[]{:S(2)}, u32[]{:S(2)}) async-start(bf16[16,8,4096]{2,1,0:T(8,128)(2,1)} %scatter_fusion), calls=%async_computation | async-start | bytes 2097152 | tf_op jit(solution)/shard_map/all_to_all | solution.py:145
  22.7 2.0 collective-permute-start
  25.5 1.4 bitcast_multiply_fusion
  26.9 2.5 sort.17
  29.5 1.1 broadcast.168.clone
  30.6 3.0 scatter_fusion.1
  33.6 26.3 %all-to-all-done = bf16[16,8,4096]{2,1,0:T(8,128)(2,1)S(1)} async-done(((bf16[16,8,4096]{2,1,0:T(8,128)(2,1)}), bf16[16,8,4096]{2,1,0:T(8,128)(2,1)S(1)}, u32[]{:S(2)}, u32[]{:S(2)}) %all-to-all-start) | async-done | bytes 1048608 | tf_op jit(solution)/shard_map/all_to_all | solution.py:145
  59.9 3.6 all-to-all-start.1
  63.5 2.0 collective-permute-start.1
  65.9 24.3 %collective-permute-done.1 = bf16[2,1,128,512]{3,2,0,1:T(8,128)(2,1)S(1)} collective-permute-done((bf16[2,1,128,512]{3,2,0,1:T(8,128)(2,1)S(1)}, bf16[2,1,128,512]{3,2,0,1:T(8,128)(2,1)S(1)}, u32[]{:S(2)}, u32[]{:S(2)}) %collective-permute-start.1) | collective-permute-done | bytes 262176 | tf_op jit(solution)/shard_map/ppermute | solution.py:24
  90.3 1.1 copy.62
  91.4 4.6 %collective-permute-start.2 = (bf16[4,1,128,512]{2,0,3,1:T(4,128)(2,1)}, bf16[4,1,128,512]{2,0,3,1:T(4,128)(2,1)}, u32[]{:S(2)}, u32[]{:S(2)}) collective-permute-start(bf16[4,1,128,512]{2,0,3,1:T(4,128)(2,1)} %copy.62), channel_id=1, source_target_pairs={{0,4},{1,5},{2,6},{3,7},{4,0},{5,1},{6,2},{7,3},{8,12},{9,13},{10,... | collective-permute-start | bytes 1572872 | tf_op jit(solution)/shard_map/ppermute | solution.py:24
  96.8 1.1 broadcast.168.clone.2
  97.9 3.4 scatter_fusion.2
  101.5 1.1 copy.63
  102.6 23.8 %collective-permute-done.2 = bf16[4,1,128,512]{2,0,3,1:T(4,128)(2,1)} collective-permute-done((bf16[4,1,128,512]{2,0,3,1:T(4,128)(2,1)}, bf16[4,1,128,512]{2,0,3,1:T(4,128)(2,1)}, u32[]{:S(2)}, u32[]{:S(2)}) %collective-permute-start.2) | collective-permute-done | bytes 524320 | tf_op jit(solution)/shard_map/ppermute | solution.py:24
  126.4 2.0 pad_maximum_fusion
  128.8 1.2 reshape_squeeze_reshape_transpose_reshape.3
  130.7 4.3 %all-to-all-start.2 = ((bf16[16,8,4096]{2,1,0:T(8,128)(2,1)}), bf16[16,8,4096]{2,1,0:T(8,128)(2,1)}, u32[]{:S(2)}, u32[]{:S(2)}) async-start(bf16[16,8,4096]{2,1,0:T(8,128)(2,1)} %scatter_fusion.2), calls=%async_computation.2 | async-start | bytes 2097152 | tf_op jit(solution)/shard_map/all_to_all | solution.py:147
  135.2 1.8 gather_fusion.2
  137.0 1.2 fusion.26
  138.9 13.6 %while.28 = (s32[]{:T(128)}, f32[4,8,128]{2,1,0:T(8,128)S(1)}, f32[4,8,128]{2,1,0:T(8,128)S(1)}, s32[2]{0:T(128)S(1)}, s32[12]{0:T(128)S(1)}, /*index=5*/s32[128...) while((s32[]{:T(128)}, f32[4,8,128]{2,1,0:T(8,128)S(1)}, ...), condition=%wide.region_9.11_spmd.clone, body=%wide.region_5.10_spmd.clone.sunk | while | flops 553883776 | bytes 20869912 | solution.py:68
  140.8 1.1 constant_dynamic-slice_fusion.6
  142.1 1.4 fusion.64
  143.6 2.2 select_reduce_fusion.2
  147.6 1.1 constant_dynamic-slice_fusion.6
  148.9 1.4 fusion.64
  150.4 2.2 select_reduce_fusion.2
  152.6 1.4 copy.90
  154.0 1.4 copy.68
  155.4 5.6 %all-to-all-done.2 = bf16[16,8,4096]{2,1,0:T(8,128)(2,1)} async-done(((bf16[16,8,4096]{2,1,0:T(8,128)(2,1)}), bf16[16,8,4096]{2,1,0:T(8,128)(2,1)}, u32[]{:S(2)}, u32[]{:S(2)}) %all-to-all-start.2) | async-done | bytes 1048608 | tf_op jit(solution)/shard_map/all_to_all | solution.py:147
  161.0 1.8 gather_fusion.3
  164.4 1.5 broadcast.166.clone
  165.9 1.4 broadcast.166
  167.3 58.4 %while.29 = (s32[]{:T(128)}, f32[128,4,8,128]{0,3,2,1:T(8,128)}, f32[1024,4,128]{2,0,1:T(8,128)}, f32[1024,4,128]{2,0,1:T(8,128)}, bf16[2,512,512]{1,2,0:T(8,128...) while((s32[]{:T(128)}, f32[128,4,8,128]{0,3,2,1:T(8,128)}, ...), condition=%wide.region_15.17_spmd.clone, body=%wide.region_13.16_spmd.clone.sunk | while | flops 2713405440 | bytes 80475096 | solution.py:68
  171.5 1.1 constant_dynamic-slice_fusion.8
  172.8 1.2 constant_dynamic-slice_fusion.7
  174.0 1.3 fusion.76
  175.3 2.1 fusion.79
  177.4 3.6 fusion.77
  181.0 1.3 fusion.78
  182.3 2.3 bitcast_add_fusion.2
  184.6 5.9 %dynamic_update_slice.10 = f32[1024,4,128]{2,0,1:T(8,128)} dynamic-update-slice(f32[1024,4,128]{2,0,1:T(8,128)} %get-tuple-element.564, f32[512,4,128]{2,0,1:T(8,128)S(1)} %fusion.78, s32[]{:T(128)S(6)} %select_n.202, s32[]{:T(128)} %constant.75.clone.1..sunk.1, s32[]{:T(128)} %constant.75.clone.1..sunk.1) | dynamic-update-slice | bytes 2097156 | tf_op jit(solution)/shard_map/while/body/eval_jaxpr/dynamic_update_slice | solution.py:198
  190.5 5.9 %dynamic_update_slice.11 = f32[1024,4,128]{2,0,1:T(8,128)} dynamic-update-slice(f32[1024,4,128]{2,0,1:T(8,128)} %get-tuple-element.565, f32[512,4,128]{2,0,1:T(8,128)S(1)} %fusion.79, s32[]{:T(128)S(6)} %select_n.202, s32[]{:T(128)} %constant.75.clone.1..sunk.1, s32[]{:T(128)} %constant.75.clone.1..sunk.1) | dynamic-update-slice | bytes 2097156 | tf_op jit(solution)/shard_map/while/body/eval_jaxpr/dynamic_update_slice | solution.py:200
  200.6 1.1 constant_dynamic-slice_fusion.8
  201.9 1.2 constant_dynamic-slice_fusion.7
  203.1 1.3 fusion.76
  204.4 2.1 fusion.79
  206.5 3.6 fusion.77
  210.1 1.3 fusion.78
  211.4 3.9 %bitcast_add_fusion.2 = f32[128,4,8,128]{0,3,2,1:T(8,128)} fusion(f32[128,4,8,128]{0,3,2,1:T(8,128)} %get-tuple-element.563, bf16[512,4,128,1]{0,2,3,1:T(8,128)(2,1)S(1)} %bitcast.175, bf16[4,8,128,512]{2,3,1,0:T(8,128)(2,1)S(1)} %fusion.77, pred[]{:T(512)S(6)} %compare.25), kind=kOutput, calls=%fused_computation.31.clone.1 | convolution fusion | flops 537919488 | bytes 8912897 | tf_op jit(solution)/shard_map/while/body/eval_jaxpr/gsrn,ngd->rgsd/dot_general | solution.py:94
  215.3 5.2 %dynamic_update_slice.10 = f32[1024,4,128]{2,0,1:T(8,128)} dynamic-update-slice(f32[1024,4,128]{2,0,1:T(8,128)} %get-tuple-element.564, f32[512,4,128]{2,0,1:T(8,128)S(1)} %fusion.78, s32[]{:T(128)S(6)} %select_n.202, s32[]{:T(128)} %constant.75.clone.1..sunk.1, s32[]{:T(128)} %constant.75.clone.1..sunk.1) | dynamic-update-slice | bytes 2097156 | tf_op jit(solution)/shard_map/while/body/eval_jaxpr/dynamic_update_slice | solution.py:198
  220.5 5.2 %dynamic_update_slice.11 = f32[1024,4,128]{2,0,1:T(8,128)} dynamic-update-slice(f32[1024,4,128]{2,0,1:T(8,128)} %get-tuple-element.565, f32[512,4,128]{2,0,1:T(8,128)S(1)} %fusion.79, s32[]{:T(128)S(6)} %select_n.202, s32[]{:T(128)} %constant.75.clone.1..sunk.1, s32[]{:T(128)} %constant.75.clone.1..sunk.1) | dynamic-update-slice | bytes 2097156 | tf_op jit(solution)/shard_map/while/body/eval_jaxpr/dynamic_update_slice | solution.py:200
  226.9 38.4 %psum.7 = f32[]{:T(128)} all-reduce(f32[]{:T(128)} %convert_reduce_fusion.4), channel_id=1, replica_groups=mesh['grp'=4,'ctx'=8] {'grp','ctx'}, use_global_device_ids=true, to_apply=%region_17.19 | all-reduce | flops 1 | bytes 8 | tf_op jit(solution)/shard_map/psum | solution.py:119
  266.0 1.9 multiply_convert_fusion
  267.9 1.3 copy.80
  269.2 24.1 %reduce-scatter.5.cloned.1.call-done = f32[128,4,128]{2,0,1:T(8,128)} async-done(((f32[1024,4,128]{2,0,1:T(8,128)}), f32[128,4,128]{2,0,1:T(8,128)}) %reduce-scatter.5.cloned.1.call-update) | async-done | bytes 262160 | tf_op jit(solution)/shard_map/reduce_scatter | solution.py:213
  293.4 70.6 %reduce-scatter.3.cloned.1.call-done = f32[128,4,128]{2,0,1:T(8,128)} async-done(((f32[1024,4,128]{2,0,1:T(8,128)}), f32[128,4,128]{2,0,1:T(8,128)}) %reduce-scatter.3.cloned.1.call-update) | async-done | bytes 262160 | tf_op jit(solution)/shard_map/reduce_scatter | solution.py:212
  364.0 1.1 multiply_convert_fusion.1
  365.2 0.7 reshape.215
  366.0 0.7 reshape.214
  (111 shorter events, 15.9 us)
Async XLA Ops:
  7.2 26.4 %copy-start.4 = (bf16[1,128,512]{2,1,0:T(8,128)(2,1)S(1)}, bf16[1,128,512]{2,1,0:T(8,128)(2,1)}, u32[]{:S(2)}) copy-start(bf16[1,128,512]{2,1,0:T(8,128)(2,1)} %param.15) | copy-start | bytes 393220
  7.2 19.8 %copy-start.5 = (s32[1,128]{1,0:T(1,128)S(1)}, s32[1,128]{1,0:T(1,128)}, u32[]{:S(2)}) copy-start(s32[1,128]{1,0:T(1,128)} %param.21) | copy-start | bytes 1540
  7.2 58.4 %copy-start.6 = (s32[1,12]{1,0:T(1,128)S(1)}, s32[1,12]{1,0:T(1,128)}, u32[]{:S(2)}) copy-start(s32[1,12]{1,0:T(1,128)} %param.20) | copy-start | bytes 148
  7.2 131.7 %all-gather.3.cloned.1.call-start = ((), (), s32[]{:S(2)}) async-start(), calls=%async_computation.5 | async-start | bytes 1179648 | tf_op jit(solution)/shard_map/all_gather | solution.py:170
  15.4 44.5 %all-to-all-start = ((bf16[16,8,4096]{2,1,0:T(8,128)(2,1)}), bf16[16,8,4096]{2,1,0:T(8,128)(2,1)S(1)}, u32[]{:S(2)}, u32[]{:S(2)}) async-start(bf16[16,8,4096]{2,1,0:T(8,128)(2,1)} %scatter_fusion), calls=%async_computation | async-start | bytes 2097152 | tf_op jit(solution)/shard_map/all_to_all | solution.py:145
  22.7 141.7 %all-gather.5.cloned.1.call-start = ((), (), s32[]{:S(2)}) async-start(), calls=%async_computation.6 | async-start | bytes 1179648 | tf_op jit(solution)/shard_map/all_gather | solution.py:208
  22.7 10.8 %collective-permute-start = (bf16[1,1,128,512]{3,2,1,0:T(8,128)(2,1)}, bf16[1,1,128,512]{3,2,1,0:T(8,128)(2,1)S(1)}, u32[]{:S(2)}, u32[]{:S(2)}) collective-permute-start(bf16[1,1,128,512]{3,2,1,0:T(8,128)(2,1)} %bitcast.188), channel_id=1, source_target_pairs={{0,1},{1,0},{2,3},{3,2},{4,5},{5,4},{6,7},{7,6},{8,9},{9,8},{10,11... | collective-permute-start | bytes 393224 | tf_op jit(solution)/shard_map/ppermute | solution.py:24
  59.9 70.7 %all-to-all-start.1 = ((bf16[16,8,4096]{2,1,0:T(8,128)(2,1)}), bf16[16,8,4096]{2,1,0:T(8,128)(2,1)S(1)}, u32[]{:S(2)}, u32[]{:S(2)}) async-start(bf16[16,8,4096]{2,1,0:T(8,128)(2,1)} %scatter_fusion.1), calls=%async_computation.1 | async-start | bytes 2097152 | tf_op jit(solution)/shard_map/all_to_all | solution.py:146
  63.5 26.6 %collective-permute-start.1 = (bf16[2,1,128,512]{3,2,0,1:T(8,128)(2,1)S(1)}, bf16[2,1,128,512]{3,2,0,1:T(8,128)(2,1)S(1)}, u32[]{:S(2)}, u32[]{:S(2)}) collective-permute-start(bf16[2,1,128,512]{3,2,0,1:T(8,128)(2,1)S(1)} %get-tuple-element.357), channel_id=1, source_target_pairs={{0,2},{1,3},{2,0},{3,1},{4,6},{5,7},{6,4},{7,5},{8,10},{9,11},{10,... | collective-permute-start | bytes 786440 | tf_op jit(solution)/shard_map/ppermute | solution.py:24
  91.4 35.0 %collective-permute-start.2 = (bf16[4,1,128,512]{2,0,3,1:T(4,128)(2,1)}, bf16[4,1,128,512]{2,0,3,1:T(4,128)(2,1)}, u32[]{:S(2)}, u32[]{:S(2)}) collective-permute-start(bf16[4,1,128,512]{2,0,3,1:T(4,128)(2,1)} %copy.62), channel_id=1, source_target_pairs={{0,4},{1,5},{2,6},{3,7},{4,0},{5,1},{6,2},{7,3},{8,12},{9,13},{10,... | collective-permute-start | bytes 1572872 | tf_op jit(solution)/shard_map/ppermute | solution.py:24
  130.6 4.3 %copy-start.2 = (bf16[16,8,4096]{2,1,0:T(8,128)(2,1)}, bf16[16,8,4096]{2,1,0:T(8,128)(2,1)S(1)}, u32[]{:S(2)}) copy-start(bf16[16,8,4096]{2,1,0:T(8,128)(2,1)S(1)} %all-to-all-done.1) | copy-start | bytes 3145732
  130.7 30.3 %all-to-all-start.2 = ((bf16[16,8,4096]{2,1,0:T(8,128)(2,1)}), bf16[16,8,4096]{2,1,0:T(8,128)(2,1)}, u32[]{:S(2)}, u32[]{:S(2)}) async-start(bf16[16,8,4096]{2,1,0:T(8,128)(2,1)} %scatter_fusion.2), calls=%async_computation.2 | async-start | bytes 2097152 | tf_op jit(solution)/shard_map/all_to_all | solution.py:147
  134.9 158.4 %reduce-scatter.5.cloned.1.call-start = ((), (), s32[]{:S(2)}) async-start(), calls=%async_computation.8 | async-start | bytes 2359296 | tf_op jit(solution)/shard_map/reduce_scatter | solution.py:213
  167.3 59.0 %copy-start.7 = (s32[1,128]{1,0:T(1,128)S(1)}, s32[1,128]{1,0:T(1,128)}, u32[]{:S(2)}) copy-start(s32[1,128]{1,0:T(1,128)} %param.19) | copy-start | bytes 1540
  172.8 2.6 copy-start.1
  172.8 2.6 copy-start.3
  177.4 3.6 copy-start
  201.9 2.6 copy-start.1
  201.9 2.6 copy-start.3
  206.5 3.6 copy-start
  225.7 138.3 %reduce-scatter.3.cloned.1.call-start = ((), (), s32[]{:S(2)}) async-start(), calls=%async_computation.7 | async-start | bytes 2359296 | tf_op jit(solution)/shard_map/reduce_scatter | solution.py:212
Sparse Core Ops, SparseCore 0:
  10.2 50.5 all-gather.2
  62.9 56.6 all-gather.4
  225.8 67.5 reduce-scatter.4
  296.8 67.1 reduce-scatter.2
